TPU v7x, 32 devices: a whole 2x2x4 slice. The times are simulated.
32 devices in a mesh: grp: 4 (over y, core), seq: 8 (over z, x).
Axes of the slice: x: 2, y: 2, z: 4, core: 2. Of those that a mesh axis runs over, the one named last changes fastest.
Arguments:
- query_heads: bfloat16 [32, 12, 128, 128], P('grp', None, 'seq'), may hold values from -40 to 40
- key_heads: bfloat16 [32, 12, 128, 128], P('grp', None, 'seq'), may hold values from -40 to 40
- value_heads: bfloat16 [32, 12, 128, 128], P('grp', None, 'seq'), may hold values from -8 to 8
- residual: bfloat16 [32, 128, 1536], P('grp', 'seq'), may hold values from -16 to 16
- modulation: bfloat16 [32, 4, 1536], P('grp'), may hold values from 0.099609375 to 1.8984375
- router: bfloat16 [1536, 8], replicated, may hold values from -0.15625 to 0.15625
- up_proj: bfloat16 [8, 2048, 1536], P('seq', 'grp'), may hold values from -0.15625 to 0.15625
- down_proj: bfloat16 [8, 2048, 1536], P('seq', 'grp'), may hold values from -0.125 to 0.125
- expert_ids: int32 [4, 8, 128, 2], P('grp', 'seq'), may hold values from 0 to 7, all different within a row; in each aligned block of 128 rows (0 to 127, 128 to 255, ..., all dimensions but the last counted through in order) at most 64 rows name the same one
Outputs:
- output: bfloat16 [32, 128, 1536], P('grp', 'seq')
Inputs may be any that keep to these rules, and one draw needn't show every extreme that they name: `expert_ids`: each token names two different experts. Among the 128 tokens of one device no expert is named by more than 64 of them, and in every draw some device names some expert exactly 64 times.
All inputs are finite; a program needn't handle non-finite values.
Results may differ from a plain program's by a relative error of at most 0.012.
Values may be sent and summed in bfloat16 or wider, within the bound.
A program may use at most 64 MiB of HBM per device.

v0:
```python
import math

import jax
import jax.numpy as jnp
from jax import lax
from jax.sharding import PartitionSpec as P

norm_eps = 1e-06


def attend_items(pieces):
    queries, key_rows, values = pieces
    item_count = queries.shape[1]
    length = queries.shape[2]
    head_width = queries.shape[3]
    block_rows = min(length, 512)
    block_count = length // block_rows
    scale_factor_term = 1.0 / math.sqrt(head_width)
    query_blocks = (
        queries[0].reshape(item_count, block_count, block_rows, head_width).transpose(1, 0, 2, 3)
    )

    def one_block(query_block):
        attention_scores = (
            jnp.einsum("kld,kmd->klm", query_block, key_rows[0], preferred_element_type=jnp.float32)
            * scale_factor_term
        )
        weight_matrix_set = jax.nn.softmax(attention_scores, axis=-1).astype(jnp.bfloat16)
        return jnp.einsum(
            "klm,kmd->kld", weight_matrix_set, values[0], preferred_element_type=jnp.float32
        ).astype(jnp.bfloat16)

    outputs = lax.map(one_block, query_blocks)
    merged = outputs.transpose(1, 0, 2, 3).reshape(1, item_count, length, head_width)
    return lax.all_to_all(merged, "seq", split_axis=2, concat_axis=0, tiled=True)


def per_device(
    query_heads,
    key_heads,
    value_heads,
    residual,
    modulation,
    router,
    up_proj,
    down_proj,
    expert_ids,
):
    seqs_dev, head_count, len_dev, head_width = query_heads.shape
    group_indices = lax.axis_size("seq")
    pair_count = seqs_dev * head_count // group_indices
    tok_dev = seqs_dev * len_dev
    model_width = head_count * head_width

    def arrange(array):
        return array.reshape(group_indices, pair_count, len_dev, head_width)

    attended = attend_items(
        (
            lax.all_to_all(arrange(query_heads), "seq", split_axis=0, concat_axis=2, tiled=True),
            lax.all_to_all(arrange(key_heads), "seq", split_axis=0, concat_axis=2, tiled=True),
            lax.all_to_all(arrange(value_heads), "seq", split_axis=0, concat_axis=2, tiled=True),
        )
    )
    attn_tok = (
        attended.reshape(seqs_dev, head_count, len_dev, head_width)
        .transpose(0, 2, 1, 3)
        .reshape(seqs_dev, len_dev, model_width)
    )
    modulators = modulation.astype(jnp.float32)
    stream = (
        residual.astype(jnp.float32) + modulators[:, 0:1, :] * attn_tok.astype(jnp.float32)
    ).astype(jnp.bfloat16)
    widened = stream.astype(jnp.float32)
    center = jnp.mean(widened, axis=-1, keepdims=True)
    spread = jnp.mean(jnp.square(widened - center), axis=-1, keepdims=True)
    normed = (
        (widened - center) * lax.rsqrt(spread + norm_eps) * modulators[:, 1:2, :]
        + modulators[:, 2:3, :]
    ).astype(jnp.bfloat16)
    tokens = normed.reshape(tok_dev, model_width)
    chosen = expert_ids.reshape(tok_dev, 2)
    logits = jnp.dot(tokens, router, preferred_element_type=jnp.float32)
    picked = jnp.take_along_axis(logits, chosen, axis=1)
    lifted = jax.nn.sigmoid(picked)
    gate_mix = lifted / jnp.sum(lifted, axis=1, keepdims=True)
    experts = router.shape[1]
    capacity = 4 * tok_dev // experts
    flat_ids = chosen.reshape(-1)
    onehot = (flat_ids[:, None] == jnp.arange(experts, dtype=jnp.int32)[None, :]).astype(jnp.int32)
    running = jnp.cumsum(onehot, axis=0)
    slot_index = jnp.sum(running * onehot, axis=1) - 1
    target = (flat_ids * capacity + slot_index).reshape(tok_dev, 2)
    places = jnp.arange(experts * capacity, dtype=jnp.int32)[:, None]
    placing = ((places == target[None, :, 0]) | (places == target[None, :, 1])).astype(jnp.bfloat16)
    outbound = (
        jnp.dot(placing, tokens, preferred_element_type=jnp.float32)
        .astype(jnp.bfloat16)
        .reshape(experts, capacity, model_width)
    )
    inbound = lax.all_to_all(outbound, "seq", split_axis=0, concat_axis=0, tiled=True)
    arrived = inbound.reshape(group_indices * capacity, model_width)
    up_local = up_proj[0]
    down_local = down_proj[0]
    up_piece = lax.all_gather(up_local, "grp", axis=0, tiled=True)
    down_piece = lax.all_gather(down_local, "grp", axis=0, tiled=True)
    pre_act = lax.dot_general(
        arrived, up_piece, (((1,), (1,)), ((), ())), preferred_element_type=jnp.float32
    )
    hidden = jax.nn.gelu(pre_act).astype(jnp.bfloat16)
    summed = jnp.dot(hidden, down_piece, preferred_element_type=jnp.float32)
    results = summed.astype(jnp.bfloat16)
    returned = lax.all_to_all(
        results.reshape(group_indices, capacity, model_width),
        "seq",
        split_axis=0,
        concat_axis=0,
        tiled=True,
    )
    slots_back = returned.reshape(experts * capacity, model_width)
    fetched = slots_back[target]
    moe_sum = jnp.sum(gate_mix[:, :, None] * fetched.astype(jnp.float32), axis=1)
    output = (
        widened + modulators[:, 3:4, :] * moe_sum.reshape(seqs_dev, len_dev, model_width)
    ).astype(jnp.bfloat16)
    return output


def solution(mesh):
    return jax.shard_map(
        per_device,
        mesh=mesh,
        in_specs=(
            P("grp", None, "seq", None),
            P("grp", None, "seq", None),
            P("grp", None, "seq", None),
            P("grp", "seq", None),
            P("grp", None, None),
            P(),
            P("seq", "grp", None),
            P("seq", "grp", None),
            P("grp", "seq", None, None),
        ),
        out_specs=P("grp", "seq", None),
        check_vma=False,
    )
```

profile of v0, /device:TPU:0, one launch (start us, length us, event | category | flops | bytes accessed | tf_op | source)
XLA Modules:
  0.0 183.6 jit_solution(7341048120168785120)
XLA Ops:
  6.5 0.0 copy-start
  6.5 0.0 copy-start.3
  6.5 0.0 copy-start.2
  6.5 0.0 all-gather.5.cloned.1.call-start
  6.5 0.7 all-gather.5.cloned.1.call-update
  7.3 0.0 all-gather.7.cloned.1.call-start
  7.3 0.7 all-gather.7.cloned.1.call-update
  8.0 19.4 %all_to_all.67 = bf16[8,12,16,128]{3,2,1,0:T(8,128)(2,1)S(1)} all-to-all(bf16[8,12,16,128]{3,2,1,0:T(8,128)(2,1)} %param.9), channel_id=1, replica_groups=mesh['grp'=4,'seq'=8] {'seq'}, dimensions={0} | all-to-all | bytes 786432 | tf_op jit(solution)/shard_map/all_to_all | solution.py:60
  27.4 3.5 %all-to-all-start.1 = ((bf16[8,12,16,128]{3,2,1,0:T(8,128)(2,1)}), bf16[8,12,16,128]{3,2,1,0:T(8,128)(2,1)S(1)}, u32[]{:S(2)}, u32[]{:S(2)}) async-start(bf16[8,12,16,128]{3,2,1,0:T(8,128)(2,1)} %param.10), calls=%async_computation.1 | async-start | bytes 786432 | tf_op jit(solution)/shard_map/all_to_all | solution.py:61
  30.8 0.0 copy-done.3
  30.8 0.1 copy.52
  31.0 0.1 eq.60
  31.1 0.1 eq.56
  31.2 0.6 reduce-window.6
  31.8 0.2 slice_reduce_fusion
  32.1 10.0 %all-to-all-done.1 = bf16[8,12,16,128]{3,2,1,0:T(8,128)(2,1)S(1)} async-done(((bf16[8,12,16,128]{3,2,1,0:T(8,128)(2,1)}), bf16[8,12,16,128]{3,2,1,0:T(8,128)(2,1)S(1)}, u32[]{:S(2)}, u32[]{:S(2)}) %all-to-all-start.1) | async-done | bytes 393248 | tf_op jit(solution)/shard_map/all_to_all | solution.py:61
  42.1 3.6 %all-to-all-start.2 = ((bf16[8,12,16,128]{3,2,1,0:T(8,128)(2,1)}), bf16[8,12,16,128]{3,2,1,0:T(8,128)(2,1)S(1)}, u32[]{:S(2)}, u32[]{:S(2)}) async-start(bf16[8,12,16,128]{3,2,1,0:T(8,128)(2,1)} %param.11), calls=%async_computation.2 | async-start | bytes 786432 | tf_op jit(solution)/shard_map/all_to_all | solution.py:62
  45.8 0.1 fusion.39
  45.9 0.1 sub.37
  46.0 0.1 copy.57
  46.1 0.0 copy-done.2
  46.2 10.7 %all-to-all-done.2 = bf16[8,12,16,128]{3,2,1,0:T(8,128)(2,1)S(1)} async-done(((bf16[8,12,16,128]{3,2,1,0:T(8,128)(2,1)}), bf16[8,12,16,128]{3,2,1,0:T(8,128)(2,1)S(1)}, u32[]{:S(2)}, u32[]{:S(2)}) %all-to-all-start.2) | async-done | bytes 393248 | tf_op jit(solution)/shard_map/all_to_all | solution.py:62
  56.9 0.5 fusion.49
  57.4 0.4 convolution_multiply_fusion
  57.8 0.0 copy-start.1
  57.8 0.4 fusion.20
  58.2 1.1 copy.51
  59.3 3.7 %all-to-all-start.3 = ((bf16[1,12,128,128]{3,1,0,2:T(8,128)(2,1)}), bf16[1,12,128,128]{3,1,0,2:T(8,128)(2,1)S(1)}, u32[]{:S(2)}, u32[]{:S(2)}) async-start(bf16[1,12,128,128]{3,1,0,2:T(8,128)(2,1)} %copy.51), calls=%async_computation.3 | async-start | bytes 1048576 | tf_op jit(solution)/shard_map/all_to_all | solution.py:35
  63.0 13.9 %all-to-all-done.3 = bf16[1,12,128,128]{3,1,0,2:T(8,128)(2,1)S(1)} async-done(((bf16[1,12,128,128]{3,1,0,2:T(8,128)(2,1)}), bf16[1,12,128,128]{3,1,0,2:T(8,128)(2,1)S(1)}, u32[]{:S(2)}, u32[]{:S(2)}) %all-to-all-start.3) | async-done | bytes 393248 | tf_op jit(solution)/shard_map/all_to_all | solution.py:35
  76.9 0.1 convert_bitcast_fusion
  77.0 0.1 reshape.181
  77.1 0.0 copy-done.1
  77.1 0.2 convert_reduce_fusion
  77.3 0.3 fusion.25
  77.6 0.4 fusion.28
  78.0 0.6 convolution_convert_fusion
  78.5 40.2 %all_to_all.68 = bf16[8,64,1536]{2,1,0:T(8,128)(2,1)S(1)} all-to-all(bf16[8,64,1536]{2,1,0:T(8,128)(2,1)S(1)} %bitcast.92), channel_id=1, replica_groups=mesh['grp'=4,'seq'=8] {'seq'}, dimensions={0} | all-to-all | bytes 3145728 | tf_op jit(solution)/shard_map/all_to_all | solution.py:101
  118.7 0.0 all-gather.5.cloned.1.call-done
  118.7 0.0 all-gather.7.cloned.1.call-done
  118.7 12.5 %fusion.13 = bf16[512,1536]{1,0:T(8,128)(2,1)} fusion(bf16[1,2048,1536]{2,1,0:T(8,128)(2,1)} %all-gather.7.cloned.1.call-done, bf16[512,1536]{1,0:T(8,128)(2,1)S(1)} %bitcast.98, bf16[1,2048,1536]{2,1,0:T(8,128)(2,1)} %all-gather.5.cloned.1.call-done), kind=kOutput, calls=%fused_computation.16 | convolution fusion | flops 6452674560 | bytes 15728640 | tf_op jit(solution)/shard_map/dot_general | solution.py:111
  131.2 3.8 %all-to-all-start.5 = ((bf16[8,64,1536]{2,1,0:T(8,128)(2,1)}), bf16[8,64,1536]{2,1,0:T(8,128)(2,1)S(1)}, u32[]{:S(2)}, u32[]{:S(2)}) async-start(bf16[8,64,1536]{2,1,0:T(8,128)(2,1)} %bitcast.97), calls=%async_computation.5 | async-start | bytes 3145728 | tf_op jit(solution)/shard_map/all_to_all | solution.py:113
  135.0 0.1 sub.38
  135.2 0.1 reshape.191
  135.3 0.1 reshape.185
  135.5 0.0 copy-done
  135.5 0.2 fusion.50
  135.7 1.4 gather_fusion.1
  137.1 0.1 reshape.194
  137.2 0.1 copy.53
  137.3 0.1 copy.54
  137.5 33.9 %all-to-all-done.5 = bf16[8,64,1536]{2,1,0:T(8,128)(2,1)S(1)} async-done(((bf16[8,64,1536]{2,1,0:T(8,128)(2,1)}), bf16[8,64,1536]{2,1,0:T(8,128)(2,1)S(1)}, u32[]{:S(2)}, u32[]{:S(2)}) %all-to-all-start.5) | async-done | bytes 1572896 | tf_op jit(solution)/shard_map/all_to_all | solution.py:113
  171.4 1.3 gather_fusion
  172.6 1.0 reshape.201
  173.6 2.3 %multiply_reduce_fusion = f32[128,1536]{1,0:T(8,128)S(1)} fusion(f32[128,2,1536]{2,1,0:T(2,128)S(1)} %reshape.201, f32[128,2]{1,0:T(8,128)S(1)} %copy.54), kind=kLoop, calls=%fused_computation.18 | loop fusion | flops 589824 | bytes 2360320 | tf_op jit(solution)/shard_map/reduce_sum | solution.py:122
  175.9 0.8 fusion.29
  (17 shorter events, 0.3 us)
Async XLA Ops:
  6.5 128.9 %copy-start = (bf16[1536,8]{0,1:T(8,128)(2,1)S(1)}, bf16[1536,8]{0,1:T(8,128)(2,1)}, u32[]{:S(2)}) copy-start(bf16[1536,8]{0,1:T(8,128)(2,1)} %param.14) | copy-start | bytes 73732
  6.5 24.3 %copy-start.3 = (s32[1,1,128,2]{2,3,1,0:T(2,128)S(1)}, s32[1,1,128,2]{2,3,1,0:T(2,128)}, u32[]{:S(2)}) copy-start(s32[1,1,128,2]{2,3,1,0:T(2,128)} %param.17) | copy-start | bytes 3076
  6.5 39.5 %copy-start.2 = (bf16[8,4,1536]{2,1,0:T(4,128)(2,1)S(1)}, bf16[8,4,1536]{2,1,0:T(4,128)(2,1)}, u32[]{:S(2)}) copy-start(bf16[8,4,1536]{2,1,0:T(4,128)(2,1)} %param.13) | copy-start | bytes 294916
  6.5 112.2 %all-gather.5.cloned.1.call-start = ((), (), s32[]{:S(2)}) async-start(), calls=%async_computation.6 | async-start | bytes 7864320 | tf_op jit(solution)/shard_map/all_gather | solution.py:105
  7.3 111.4 %all-gather.7.cloned.1.call-start = ((), (), s32[]{:S(2)}) async-start(), calls=%async_computation.7 | async-start | bytes 7864320 | tf_op jit(solution)/shard_map/all_gather | solution.py:106
  27.4 14.8 %all-to-all-start.1 = ((bf16[8,12,16,128]{3,2,1,0:T(8,128)(2,1)}), bf16[8,12,16,128]{3,2,1,0:T(8,128)(2,1)S(1)}, u32[]{:S(2)}, u32[]{:S(2)}) async-start(bf16[8,12,16,128]{3,2,1,0:T(8,128)(2,1)} %param.10), calls=%async_computation.1 | async-start | bytes 786432 | tf_op jit(solution)/shard_map/all_to_all | solution.py:61
  42.1 14.7 %all-to-all-start.2 = ((bf16[8,12,16,128]{3,2,1,0:T(8,128)(2,1)}), bf16[8,12,16,128]{3,2,1,0:T(8,128)(2,1)S(1)}, u32[]{:S(2)}, u32[]{:S(2)}) async-start(bf16[8,12,16,128]{3,2,1,0:T(8,128)(2,1)} %param.11), calls=%async_computation.2 | async-start | bytes 786432 | tf_op jit(solution)/shard_map/all_to_all | solution.py:62
  57.8 19.4 %copy-start.1 = (bf16[8,16,1536]{2,1,0:T(8,128)(2,1)S(1)}, bf16[8,16,1536]{2,1,0:T(8,128)(2,1)}, u32[]{:S(2)}) copy-start(bf16[8,16,1536]{2,1,0:T(8,128)(2,1)} %param.12) | copy-start | bytes 1179652
  59.3 17.7 %all-to-all-start.3 = ((bf16[1,12,128,128]{3,1,0,2:T(8,128)(2,1)}), bf16[1,12,128,128]{3,1,0,2:T(8,128)(2,1)S(1)}, u32[]{:S(2)}, u32[]{:S(2)}) async-start(bf16[1,12,128,128]{3,1,0,2:T(8,128)(2,1)} %copy.51), calls=%async_computation.3 | async-start | bytes 1048576 | tf_op jit(solution)/shard_map/all_to_all | solution.py:35
  131.2 40.2 %all-to-all-start.5 = ((bf16[8,64,1536]{2,1,0:T(8,128)(2,1)}), bf16[8,64,1536]{2,1,0:T(8,128)(2,1)S(1)}, u32[]{:S(2)}, u32[]{:S(2)}) async-start(bf16[8,64,1536]{2,1,0:T(8,128)(2,1)} %bitcast.97), calls=%async_computation.5 | async-start | bytes 3145728 | tf_op jit(solution)/shard_map/all_to_all | solution.py:113
Sparse Core Ops, SparseCore 0:
  8.9 49.0 all-gather.4
  59.6 46.3 all-gather.6
where the time goes:
time: 184 us
  waiting for transfers between devices  70 us (38%)
  blocking collectives  59.5 us (32%)
  starting transfers between devices  14.6 us (8%)
  matrix products  14.5 us (8%)
  between operations  13.7 us (7%)
  local copies, waits for them, and re-layouts  6.48 us (4%)
  other arithmetic  4.88 us (3%)
    all_to_all x1, blocking collectives, per_device(): lax.all_to_all(outbound, 'seq', split_axis=0, concat_axis=0, tiled=True)  40.2 us
    all_to_all x1, waiting for transfers between devices, per_device(): lax.all_to_all(results.reshape(group_indices, capacity, model_width), 'se...  33.9 us
    all_to_all x1, blocking collectives, per_device(): lax.all_to_all(arrange(query_heads), 'seq', split_axis=0, concat_axis=2,...  19.4 us
    all_to_all x1, waiting for transfers between devices, attend_items(): lax.all_to_all(merged, 'seq', split_axis=2, concat_axis=0, tiled=True)  13.9 us
    dot_general x1, matrix products, per_device(): summed = jnp.dot(hidden, down_piece, preferred_element_type=jnp.float32)  12.5 us
    all_to_all x1, waiting for transfers between devices, per_device(): lax.all_to_all(arrange(value_heads), 'seq', split_axis=0, concat_axis=2,...  10.7 us
    all_to_all x1, waiting for transfers between devices, per_device(): lax.all_to_all(arrange(key_heads), 'seq', split_axis=0, concat_axis=2, ti...  10 us
    all_to_all x1, starting transfers between devices, per_device(): lax.all_to_all(results.reshape(group_indices, capacity, model_width), 'se...  3.76 us
  transfers between devices with their start and end apart: 6, of which 4 were waited for; matrix products, arithmetic and copies ran while one was open for 4% of the time, Pallas kernels for 0%

commit v1 on v0

v1 whole, which is shorter than its diff:
```python
import functools
import math

import jax
import jax.numpy as jnp
from jax import lax
from jax.experimental import pallas as pl
from jax.experimental.pallas import tpu as pltpu
from jax.sharding import PartitionSpec as P

norm_eps = 1e-06
BF = jnp.bfloat16
F32 = jnp.float32


def wait_bytes(ref, sem):
    pltpu.make_async_copy(ref, ref, sem).wait()


def remote(src, dst, send_sem, recv_sem, axis, index):
    return pltpu.make_async_remote_copy(
        src_ref=src,
        dst_ref=dst,
        send_sem=send_sem,
        recv_sem=recv_sem,
        device_id={axis: index},
        device_id_type=pl.DeviceIdType.MESH,
    )


def layer_kernel(
    n, n_grp, chunks,
    q_ref, k_ref, v_ref, res_ref, mod_ref, router_ref, up_ref, down_ref, ids_ref, idst_ref,
    out_ref,
    qkv, o_buf, att, stream, normed, slot_t, mix, outb, arr, back, weights, acc, moe,
    q_send, q_recv, a_send, a_recv, d_send, d_recv, r_send, r_recv,
    w_local, w_send, w_peer, w_sib, f_send, f_recv,
):
    me = lax.axis_index("seq")
    grp = lax.axis_index("grp")
    sib = grp + 1 - 2 * (grp % 2)
    chips = n_grp // 2
    half = n // 2
    seqs, ld, width = res_ref.shape
    pc = q_ref.shape[1]
    hd = q_ref.shape[3]
    heads = width // hd
    part = pc // chunks
    tok = seqs * ld
    cap = outb.shape[1]
    ff = weights.shape[2]
    fh = ff // 2

    def other(t):
        return (me + 1 + (half - 1 + t) % (n - 1)) % n

    def peer(t):
        return (grp + 2 * (t + 1)) % n_grp

    barrier = pltpu.get_barrier_semaphore()
    for t in range(n - 1):
        pl.semaphore_signal(
            barrier, inc=1, device_id={"seq": other(t)}, device_id_type=pl.DeviceIdType.MESH
        )
    for t in range(chips - 1):
        pl.semaphore_signal(
            barrier, inc=1, device_id={"grp": peer(t)}, device_id_type=pl.DeviceIdType.MESH
        )
    pl.semaphore_signal(barrier, inc=1, device_id={"grp": sib}, device_id_type=pl.DeviceIdType.MESH)
    pl.semaphore_wait(barrier, n - 1 + chips)

    def send_chunk(c):
        pairs = pl.ds(c * part, part)
        mine = pl.ds(pl.multiple_of(me * ld, ld), ld)

        def send_to(t, carry):
            dst = other(t)
            for i, ref in enumerate((q_ref, k_ref, v_ref)):
                remote(
                    ref.at[dst, pairs], qkv.at[i, pairs, mine], q_send, q_recv.at[c], "seq", dst
                ).start()
            return carry

        lax.fori_loop(0, n - 1, send_to, 0)
        for i, ref in enumerate((q_ref, k_ref, v_ref)):
            pltpu.make_async_copy(ref.at[me, pairs], qkv.at[i, pairs, mine], q_recv.at[c]).start()

    send_chunk(0)

    pieces = [(i, pl.ds(r * fh, fh)) for i in range(2) for r in range(2)]
    sources = (up_ref, down_ref)
    for j, (i, rows) in enumerate(pieces):
        for t in range(chips - 1):
            remote(
                sources[i].at[0, rows], weights.at[i, grp, rows], w_send,
                w_peer.at[grp // 2, j], "grp", peer(t),
            ).start()
    for c in range(1, chunks):
        send_chunk(c)
    for i in range(2):
        pltpu.make_async_copy(sources[i].at[0], weights.at[i, grp], w_local).start()
        remote(sources[i].at[0], weights.at[i, grp], w_send, w_sib, "grp", sib).start()

    experts = n
    before = (
        lax.broadcasted_iota(jnp.int32, (tok, tok), 0)
        < lax.broadcasted_iota(jnp.int32, (tok, tok), 1)
    ).astype(F32)
    row_e = lax.broadcasted_iota(jnp.int32, (experts, tok), 0)
    named_t = ((row_e == idst_ref[0:1, :]) | (row_e == idst_ref[1:2, :])).astype(F32)
    rank_t = jnp.dot(named_t, before, preferred_element_type=F32)
    slot_t[...] = jnp.where(named_t > 0.0, rank_t, -1.0)

    scale = 1.0 / math.sqrt(hd)

    def attend(c, carry):
        pairs = pl.ds(c * part, part)
        wait_bytes(qkv.at[:, pairs], q_recv.at[c])
        for i in range(part):
            p = c * part + i
            s = lax.dot_general(
                qkv[0, p], qkv[1, p], (((1,), (1,)), ((), ())), preferred_element_type=F32
            )
            s = s * scale
            e = jnp.exp(s - jnp.max(s, axis=-1, keepdims=True))
            wts = (e / jnp.sum(e, axis=-1, keepdims=True)).astype(BF)
            o_buf[p] = jnp.dot(wts, qkv[2, p], preferred_element_type=F32).astype(BF)
        there = pl.ds(me * pc + c * part, part)

        def send_to(t, carry2):
            dst = other(t)
            rows = pl.ds(pl.multiple_of(dst * ld, ld), ld)
            remote(o_buf.at[pairs, rows], att.at[there], a_send, a_recv, "seq", dst).start()
            return carry2

        lax.fori_loop(0, n - 1, send_to, 0)
        mine = pl.ds(pl.multiple_of(me * ld, ld), ld)
        att[there] = o_buf[pairs, mine]
        return carry

    lax.fori_loop(0, chunks, attend, 0)
    wait_bytes(att.at[pl.ds(0, (n - 1) * pc)], a_recv)

    def normalise(b, carry):
        row = jnp.concatenate([att[b * heads + h] for h in range(heads)], axis=-1)
        m = mod_ref[b].astype(F32)
        st = (res_ref[b].astype(F32) + m[0:1] * row.astype(F32)).astype(BF)
        stream[b] = st
        x = st.astype(F32)
        center = jnp.mean(x, axis=-1, keepdims=True)
        d = x - center
        spread = jnp.mean(d * d, axis=-1, keepdims=True)
        normed[b] = (d * lax.rsqrt(spread + norm_eps) * m[1:2] + m[2:3]).astype(BF)
        return carry

    lax.fori_loop(0, seqs, normalise, 0)
    tokens = normed[...].reshape(tok, width)

    def pack(e):
        place = lax.broadcasted_iota(jnp.int32, (cap, tok), 0).astype(F32)
        hot = (place == slot_t[pl.ds(e, 1), :]).astype(BF)
        return jnp.dot(hot, normed[...].reshape(tok, width), preferred_element_type=F32).astype(BF)

    def dispatch(t, carry):
        dst = other(t)
        outb[dst] = pack(dst)
        remote(outb.at[dst], arr.at[me], d_send, d_recv.at[me // half], "seq", dst).start()
        return carry

    lax.fori_loop(0, n - 1, dispatch, 0)
    arr[me] = pack(me)

    after = (
        lax.broadcasted_iota(jnp.int32, (tok, tok), 1)
        < lax.broadcasted_iota(jnp.int32, (tok, tok), 0)
    ).astype(F32)
    col_e = lax.broadcasted_iota(jnp.int32, (tok, experts), 1)
    named = ((col_e == ids_ref[:, 0:1]) | (col_e == ids_ref[:, 1:2])).astype(F32)
    slot = jnp.where(named > 0.0, jnp.dot(after, named, preferred_element_type=F32), -1.0)
    logits = jnp.dot(tokens, router_ref[...], preferred_element_type=F32)
    lifted = jnp.where(named > 0.0, jax.nn.sigmoid(logits), 0.0)
    gate = lifted / jnp.sum(lifted, axis=1, keepdims=True)
    gate_hi = gate.astype(BF)
    gate_lo = (gate - gate_hi.astype(F32)).astype(BF)
    rows_all = experts * cap
    wide = lax.broadcasted_iota(jnp.int32, (experts, rows_all), 1)
    first = lax.broadcasted_iota(jnp.int32, (experts, rows_all), 0) * cap
    spread_e = ((wide >= first) & (wide < first + cap)).astype(BF)
    slot_all = jnp.dot(slot.astype(BF), spread_e, preferred_element_type=F32)
    place_all = (lax.broadcasted_iota(jnp.int32, (tok, rows_all), 1) % cap).astype(F32)
    here = slot_all == place_all
    hi_all = jnp.dot(gate_hi, spread_e, preferred_element_type=F32)
    lo_all = jnp.dot(gate_lo, spread_e, preferred_element_type=F32)
    mix[0] = jnp.where(here, hi_all, 0.0).astype(BF)
    mix[1] = jnp.where(here, lo_all, 0.0).astype(BF)

    for j, (i, rows) in enumerate(pieces):
        for t in range(chips - 1):
            g = peer(t)
            wait_bytes(weights.at[i, g, rows], w_peer.at[g // 2, j])
            piece = weights.at[i, g, rows]
            remote(piece, piece, f_send, f_recv, "grp", sib).start()
    for i in range(2):
        wait_bytes(weights.at[i, grp], w_local)
    wait_bytes(weights.at[:, pl.ds(0, 1)], w_sib)
    wait_bytes(weights.at[:, pl.ds(0, chips - 1)], f_recv)

    my_half = me // half
    far = 1 - my_half
    wait_bytes(arr.at[pl.ds(0, half)], d_recv.at[far])
    for step in range(2):
        side = far if step == 0 else my_half
        if step == 1:
            wait_bytes(arr.at[pl.ds(0, half - 1)], d_recv.at[my_half])
        block = pl.ds(side * half, half)

        def expert(g, carry, block=block):
            x = arr[block].reshape(half * cap, width)
            u = lax.dot_general(
                x, weights[0, g], (((1,), (1,)), ((), ())), preferred_element_type=F32
            )
            inner = math.sqrt(2.0 / math.pi) * (u + 0.044715 * (u * u * u))
            hidden = (0.5 * u * (1.0 + jnp.tanh(inner))).astype(BF)
            add = jnp.dot(hidden, weights[1, g], preferred_element_type=F32)
            acc[...] = jnp.where(g == 0, add, acc[...] + add)
            return carry

        acc[...] = jnp.zeros_like(acc)
        lax.fori_loop(0, n_grp, expert, 0)
        outcome = acc[...].astype(BF).reshape(half, cap, width)
        arr[block] = outcome
        for i in range(half):
            dst = side * half + (me + i) % half

            def go(dst=dst):
                remote(
                    arr.at[dst], back.at[me], r_send, r_recv.at[my_half], "seq", dst
                ).start()

            if step == 0:
                go()
            elif i > 0:
                go()
            else:
                back[me] = arr[me]

    for step in range(2):
        side = my_half if step == 0 else far
        count = half - 1 if step == 0 else half
        wait_bytes(back.at[pl.ds(0, count)], r_recv.at[side])
        rows = back[pl.ds(side * half, half)].reshape(half * cap, width)
        lanes = pl.ds(pl.multiple_of(side * (half * cap), half * cap), half * cap)
        add = jnp.dot(mix[0, :, lanes], rows, preferred_element_type=F32)
        add = add + jnp.dot(mix[1, :, lanes], rows, preferred_element_type=F32)
        moe[...] = add if step == 0 else moe[...] + add

    def finish(b, carry):
        m = mod_ref[b].astype(F32)
        rows = moe[pl.ds(pl.multiple_of(b * ld, ld), ld), :]
        out_ref[b] = (stream[b].astype(F32) + m[3:4] * rows).astype(BF)
        return carry

    lax.fori_loop(0, seqs, finish, 0)

    wait_bytes(qkv.at[:, :, pl.ds(0, (n - 1) * ld)], q_send)
    wait_bytes(att.at[pl.ds(0, (n - 1) * pc)], a_send)
    wait_bytes(outb.at[pl.ds(0, n - 1)], d_send)
    wait_bytes(back.at[pl.ds(0, n - 1)], r_send)
    wait_bytes(weights.at[:, pl.ds(0, chips)], w_send)
    wait_bytes(weights.at[:, pl.ds(0, chips - 1)], f_send)


def per_device(
    query_heads, key_heads, value_heads, residual, modulation, router, up_proj, down_proj,
    expert_ids,
):
    seqs, heads, ld, hd = query_heads.shape
    n = lax.axis_size("seq")
    n_grp = lax.axis_size("grp")
    pc = seqs * heads // n
    chunks = 3 if pc % 3 == 0 else 1
    tok = seqs * ld
    width = heads * hd
    experts = router.shape[1]
    cap = 4 * tok // experts
    ff = up_proj.shape[1]
    half = n // 2

    def arrange(array):
        return array.reshape(n, pc, ld, hd)

    ids = expert_ids.reshape(tok, 2)
    any_spec = pl.BlockSpec(memory_space=pl.ANY)
    vmem = pl.BlockSpec(memory_space=pltpu.VMEM)
    dma = pltpu.SemaphoreType.DMA
    return pl.pallas_call(
        functools.partial(layer_kernel, n, n_grp, chunks),
        out_shape=jax.ShapeDtypeStruct((seqs, ld, width), BF),
        in_specs=[any_spec] * 3 + [vmem] * 3 + [any_spec] * 2 + [vmem] * 2,
        out_specs=vmem,
        scratch_shapes=[
            pltpu.VMEM((3, pc, n * ld, hd), BF),
            pltpu.VMEM((pc, n * ld, hd), BF),
            pltpu.VMEM((n * pc, ld, hd), BF),
            pltpu.VMEM((seqs, ld, width), BF),
            pltpu.VMEM((seqs, ld, width), BF),
            pltpu.VMEM((experts, tok), F32),
            pltpu.VMEM((2, tok, experts * cap), BF),
            pltpu.VMEM((n, cap, width), BF),
            pltpu.VMEM((n, cap, width), BF),
            pltpu.VMEM((n, cap, width), BF),
            pltpu.VMEM((2, n_grp, ff, width), BF),
            pltpu.VMEM((half * cap, width), F32),
            pltpu.VMEM((tok, width), F32),
            dma, dma((chunks,)), dma, dma, dma, dma((2,)), dma, dma((2,)),
            dma, dma, dma((n_grp // 2, 4)), dma, dma, dma,
        ],
        compiler_params=pltpu.CompilerParams(
            collective_id=0, has_side_effects=True, vmem_limit_bytes=52 * 1024 * 1024
        ),
    )(
        arrange(query_heads), arrange(key_heads), arrange(value_heads), residual, modulation,
        router, up_proj, down_proj, ids, ids.T,
    )


def solution(mesh):
    return jax.shard_map(
        per_device,
        mesh=mesh,
        in_specs=(
            P("grp", None, "seq", None),
            P("grp", None, "seq", None),
            P("grp", None, "seq", None),
            P("grp", "seq", None),
            P("grp", None, None),
            P(),
            P("seq", "grp", None),
            P("seq", "grp", None),
            P("grp", "seq", None, None),
        ),
        out_specs=P("grp", "seq", None),
        check_vma=False,
    )
```

time: 184 us -> 128 us (0.70)
  Pallas kernels: 0 us -> 120 us
  waiting for transfers between devices: 70 us -> 0 us
  blocking collectives: 59.5 us -> 0 us
  starting transfers between devices: 14.6 us -> 0 us
  matrix products: 14.5 us -> 0 us
  between operations: 13.7 us -> 0.02 us
  other arithmetic: 4.88 us -> 0 us
    pallas_call x0 -> x1, Pallas kernels: none -> 120 us  [per_device(): pl.pallas_call(functools.partial(layer_kernel, n, n_grp, chunks), out_sha...]
    all_to_all x4 -> x0, waiting for transfers between devices: 68.6 us -> none  [the longest x1 33.9 us: per_device(): lax.all_to_all(results.reshape(group_indices, capacity, model_width), 'se...]
    all_to_all x2 -> x0, blocking collectives: 59.5 us -> none  [the longest x1 40.2 us: per_device(): lax.all_to_all(outbound, 'seq', split_axis=0, concat_axis=0, tiled=True)]
    all_to_all x4 -> x0, starting transfers between devices: 14.5 us -> none  [the longest x1 3.76 us: per_device(): lax.all_to_all(results.reshape(group_indices, capacity, model_width), 'se...]
    dot_general x5 -> x0, matrix products: 14 us -> none  [the longest x1 12.5 us: per_device(): summed = jnp.dot(hidden, down_piece, preferred_element_type=jnp.float32)]
    unnamed x9 -> x12, local copies, waits for them, and re-layouts: 0.13 us -> 6.96 us
    gather x5 -> x0, local copies, waits for them, and re-layouts: 2.99 us -> none  [the longest x4 1.73 us: per_device(): picked = jnp.take_along_axis(logits, chosen, axis=1)]
    reduce_sum x5 -> x0, other arithmetic: 2.85 us -> none  [the longest x1 2.29 us: per_device(): jnp.sum(gate_mix[:, :, None] * fetched.astype(jnp.float32), axis=1)]
  transfers between devices with their start and end apart: 6 -> 0, of which waited for: 4 -> 0; matrix products, arithmetic and copies ran while one was open for 4% -> 0% of each run, Pallas kernels for 0% -> 0%
where the time goes in v1:
time: 128 us
  Pallas kernels  120 us (94%)
  local copies, waits for them, and re-layouts  7.74 us (6%)
    pallas_call x1, Pallas kernels, per_device(): pl.pallas_call(functools.partial(layer_kernel, n, n_grp, chunks), out_sha...  120 us
    unnamed x12, local copies, waits for them, and re-layouts  6.96 us

profile of v1, /device:TPU:0, one launch (start us, length us, event | category | flops | bytes accessed | tf_op | source)
XLA Modules:
  0.0 128.1 jit_solution(10231337237131803877)
XLA Ops:
  0.0 0.8 copy.11.ids_ref
  0.8 1.7 %copy.10.router_ref = bf16[1536,8]{1,0:T(8,128)(2,1)} copy(bf16[1536,8]{0,1:T(8,128)(2,1)} %param.14) | data formatting | bytes 49152 | tf_op args[5]
  2.4 0.0 copy-start
  2.4 1.0 copy-done
  3.4 0.0 copy-start.1
  3.4 1.0 copy-done.1
  4.4 0.0 copy-start.2
  4.4 1.0 copy-done.2
  5.4 0.0 copy-start.3
  5.4 0.9 copy-done.3
  6.3 0.0 copy-start.4
  6.3 0.7 copy-done.4
  7.0 120.3 %shard_map.91 = bf16[8,16,1536]{2,1,0:T(8,128)(2,1)S(1)} custom-call(bf16[8,12,16,128]{3,2,1,0:T(8,128)(2,1)S(1)} %copy-done, bf16[8,12,16,128]{3,2,1,0:T(8,128)(2,1)S(1)} %copy-done.1, bf16[8,12,16,128]{3,2,1,0:T(8,128)(2,1)S(1)} %copy-done.2, bf16[8,16,1536]{2,1,0:T(8,128)(2,1)} %res_ref.1, bf16[8,4,1536]{2,1,0:T(4,128)(2,1)S(1)} %copy-done.3, ...), custom_call_target="tpu_custom_call" | custom-call | tf_op jit(solution)/shard_map/pallas_call | solution.py:296
  127.3 0.7 copy.13
Async XLA Ops:
  2.4 1.0 copy-start
  3.4 1.0 copy-start.1
  4.4 1.0 copy-start.2
  5.4 0.9 copy-start.3
  6.3 0.7 copy-start.4

commit v2 on v1

--- a/solution.py
+++ b/solution.py
@@ -30,11 +30,11 @@
 
 def layer_kernel(
     n, n_grp, chunks,
-    q_ref, k_ref, v_ref, res_ref, mod_ref, router_ref, up_ref, down_ref, ids_ref, idst_ref,
+    q_ref, k_ref, v_ref, res_ref, mod_ref, router_ref, up_ref, down_ref, idst_ref,
     out_ref,
-    qkv, o_buf, att, stream, normed, slot_t, mix, outb, arr, back, weights, acc, moe,
+    resid, qkv, o_buf, att, stream, normed, slot_t, mix, outb, arr, back, weights, acc, moe,
     q_send, q_recv, a_send, a_recv, d_send, d_recv, r_send, r_recv,
-    w_local, w_send, w_peer, w_sib, f_send, f_recv,
+    w_local, w_send, w_peer, w_sib, f_send, f_recv, res_sem,
 ):
     me = lax.axis_index("seq")
     grp = lax.axis_index("grp")
@@ -101,6 +101,8 @@
         pltpu.make_async_copy(sources[i].at[0], weights.at[i, grp], w_local).start()
         remote(sources[i].at[0], weights.at[i, grp], w_send, w_sib, "grp", sib).start()
 
+    pltpu.make_async_copy(res_ref, resid, res_sem).start()
+
     experts = n
     before = (
         lax.broadcasted_iota(jnp.int32, (tok, tok), 0)
@@ -141,10 +143,11 @@
     lax.fori_loop(0, chunks, attend, 0)
     wait_bytes(att.at[pl.ds(0, (n - 1) * pc)], a_recv)
 
+    wait_bytes(resid, res_sem)
     def normalise(b, carry):
         row = jnp.concatenate([att[b * heads + h] for h in range(heads)], axis=-1)
         m = mod_ref[b].astype(F32)
-        st = (res_ref[b].astype(F32) + m[0:1] * row.astype(F32)).astype(BF)
+        st = (resid[b].astype(F32) + m[0:1] * row.astype(F32)).astype(BF)
         stream[b] = st
         x = st.astype(F32)
         center = jnp.mean(x, axis=-1, keepdims=True)
@@ -170,15 +173,11 @@
     lax.fori_loop(0, n - 1, dispatch, 0)
     arr[me] = pack(me)
 
-    after = (
-        lax.broadcasted_iota(jnp.int32, (tok, tok), 1)
-        < lax.broadcasted_iota(jnp.int32, (tok, tok), 0)
-    ).astype(F32)
-    col_e = lax.broadcasted_iota(jnp.int32, (tok, experts), 1)
-    named = ((col_e == ids_ref[:, 0:1]) | (col_e == ids_ref[:, 1:2])).astype(F32)
-    slot = jnp.where(named > 0.0, jnp.dot(after, named, preferred_element_type=F32), -1.0)
-    logits = jnp.dot(tokens, router_ref[...], preferred_element_type=F32)
-    lifted = jnp.where(named > 0.0, jax.nn.sigmoid(logits), 0.0)
+    slot = slot_t[...].T
+    logits = lax.dot_general(
+        tokens, router_ref[...], (((1,), (1,)), ((), ())), preferred_element_type=F32
+    )
+    lifted = jnp.where(slot >= 0.0, jax.nn.sigmoid(logits), 0.0)
     gate = lifted / jnp.sum(lifted, axis=1, keepdims=True)
     gate_hi = gate.astype(BF)
     gate_lo = (gate - gate_hi.astype(F32)).astype(BF)
@@ -290,15 +289,16 @@
         return array.reshape(n, pc, ld, hd)
 
     ids = expert_ids.reshape(tok, 2)
-    any_spec = pl.BlockSpec(memory_space=pl.ANY)
+    any_spec = pl.BlockSpec(memory_space=pltpu.HBM)
     vmem = pl.BlockSpec(memory_space=pltpu.VMEM)
     dma = pltpu.SemaphoreType.DMA
     return pl.pallas_call(
         functools.partial(layer_kernel, n, n_grp, chunks),
         out_shape=jax.ShapeDtypeStruct((seqs, ld, width), BF),
-        in_specs=[any_spec] * 3 + [vmem] * 3 + [any_spec] * 2 + [vmem] * 2,
+        in_specs=[any_spec] * 4 + [vmem] * 2 + [any_spec] * 2 + [vmem],
         out_specs=vmem,
         scratch_shapes=[
+            pltpu.VMEM((seqs, ld, width), BF),
             pltpu.VMEM((3, pc, n * ld, hd), BF),
             pltpu.VMEM((pc, n * ld, hd), BF),
             pltpu.VMEM((n * pc, ld, hd), BF),
@@ -313,14 +313,14 @@
             pltpu.VMEM((half * cap, width), F32),
             pltpu.VMEM((tok, width), F32),
             dma, dma((chunks,)), dma, dma, dma, dma((2,)), dma, dma((2,)),
-            dma, dma, dma((n_grp // 2, 4)), dma, dma, dma,
+            dma, dma, dma((n_grp // 2, 4)), dma, dma, dma, dma,
         ],
         compiler_params=pltpu.CompilerParams(
-            collective_id=0, has_side_effects=True, vmem_limit_bytes=52 * 1024 * 1024
+            collective_id=0, has_side_effects=True, vmem_limit_bytes=56 * 1024 * 1024
         ),
     )(
         arrange(query_heads), arrange(key_heads), arrange(value_heads), residual, modulation,
-        router, up_proj, down_proj, ids, ids.T,
+        router.T, up_proj, down_proj, ids.T,
     )
 
 

time: 128 us -> 123 us (0.961)
  local copies, waits for them, and re-layouts: 7.74 us -> 1.77 us
    unnamed x12 -> x1, local copies, waits for them, and re-layouts: 6.96 us -> 1.77 us
where the time goes in v2:
time: 123 us
  Pallas kernels  121 us (98%)
  local copies, waits for them, and re-layouts  1.77 us (1%)
    pallas_call x1, Pallas kernels, per_device(): pl.pallas_call(functools.partial(layer_kernel, n, n_grp, chunks), out_sha...  121 us

profile of v2, /device:TPU:0, one launch (start us, length us, event | category | flops | bytes accessed | tf_op | source)
XLA Modules:
  0.0 122.5 jit_solution(5755226134829920309)
XLA Ops:
  0.0 120.8 %shard_map.91 = bf16[8,16,1536]{2,1,0:T(8,128)(2,1)} custom-call(bf16[8,12,16,128]{3,2,1,0:T(8,128)(2,1)} %q_ref.1, bf16[8,12,16,128]{3,2,1,0:T(8,128)(2,1)} %k_ref.1, bf16[8,12,16,128]{3,2,1,0:T(8,128)(2,1)} %v_ref.1, bf16[8,16,1536]{2,1,0:T(8,128)(2,1)} %res_ref.1, bf16[8,4,1536]{2,1,0:T(4,128)(2,1)} %mod_ref.1, bf16[8,1536]{1,0:T(8,128)(2,1)} %bitcast.4, ...), custom_call_target="tpu_custom_call" | custom-call | tf_op jit(solution)/shard_map/pallas_call | solution.py:295
  120.8 1.8 %copy.11 = bf16[8,16,1536]{2,1,0:T(8,128)(2,1)} copy(bf16[8,16,1536]{2,1,0:T(8,128)(2,1)} %shard_map.91) | data formatting | bytes 786432
